TPU v7x, 32 devices: a whole 2x2x4 slice. The times are simulated.
32 devices in a mesh: group: 8 (over y, x, core), tensor: 4 (over z).
Axes of the slice: x: 2, y: 2, z: 4, core: 2. Of those that a mesh axis runs over, the one named last changes fastest.
Arguments:
- latents: bfloat16 [8, 256, 3072], P('group', 'tensor'), may hold values from -6 to 6
- stored_sample: bfloat16 [8, 256, 3072], P('group', 'tensor'), may hold values from -6 to 6
- timestep: int32 [8], P('group'), may hold values from 0 to 7
- owner_map: int32 [8], replicated, may hold values from 0 to 7, each once
- mod_table: float32 [8, 3, 3072], replicated, may hold values from -3 to 3
- qkv_weight: bfloat16 [3072, 1536], P('group', 'tensor'), may hold values from -0.5412659 to 0.5412659
- out_weight: bfloat16 [512, 3072], P('tensor', 'group'), may hold values from -0.25 to 0.25
Outputs:
- mean_next: bfloat16 [8, 256, 3072], P('group', 'tensor')
- log_prob: float32 [8], P('group')
Inputs may be any that keep to these rules, and one draw needn't show every extreme that they name: `owner_map`: each index of group holds exactly one slice.
All inputs are finite; a program needn't handle non-finite values.
Results may differ from a plain program's by a relative error of at most 0.0075.
Values may be sent and summed in bfloat16 or wider, within the bound.
A program may use at most 64 MiB of HBM per device.

v0:
```python
import math

import jax
import jax.numpy as jnp
from jax import lax
from jax.sharding import PartitionSpec as P


def shards(latents, stored_sample, timestep, owner_map, mod_table, qkv_weight, out_weight):
    groups = lax.axis_size("group")
    cycle_size = lax.axis_size("tensor")
    samples, tok_local, model_width = latents.shape
    slice_rows = qkv_weight.shape[0]
    head_dim = out_weight.shape[0]
    step_count = mod_table.shape[0]
    seq_len = tok_local * cycle_size
    onehot = (timestep[:, None] == jnp.arange(step_count, dtype=jnp.int32)[None, :]).astype(
        jnp.float32
    )
    modulation = jnp.einsum("bs,scd->bcd", onehot, mod_table, precision=lax.Precision.HIGHEST)
    shift_rows = modulation[:, 0][:, None, :]
    scale_rows = modulation[:, 1][:, None, :]
    gate_rows = modulation[:, 2][:, None, :]
    latent_f = latents.astype(jnp.float32)
    centred = latent_f - jnp.mean(latent_f, axis=-1, keepdims=True)
    variance = jnp.mean(centred * centred, axis=-1, keepdims=True)
    normed = centred * lax.rsqrt(variance + 1e-06)
    modulated = (normed * (1.0 + scale_rows) + shift_rows).astype(jnp.bfloat16)
    gathered = lax.all_gather(modulated, "tensor", axis=1, tiled=True)
    flat_rows = gathered.reshape(samples * seq_len, model_width)
    matches = owner_map[None, :] == jnp.arange(groups, dtype=jnp.int32)[:, None]
    slot_of = jnp.sum(jnp.where(matches, jnp.arange(groups, dtype=jnp.int32)[None, :], 0), axis=1)
    qkv_zero = jnp.zeros((samples * seq_len, qkv_weight.shape[1]), jnp.float32)
    out_rows = out_weight.T
    placed_zero = jnp.zeros((model_width, head_dim), jnp.bfloat16)
    portions = (
        lax.all_gather(qkv_weight, "group", axis=0, tiled=True),
        lax.all_gather(out_rows, "group", axis=0, tiled=True),
    )
    row_index = jnp.arange(portions[0].shape[0], dtype=jnp.int32)
    columns = slot_of[row_index // slice_rows] * slice_rows + row_index % slice_rows
    picked = jnp.take(flat_rows, columns, axis=1)
    running = jnp.dot(picked, portions[0], preferred_element_type=jnp.float32)
    positioned = (qkv_zero, placed_zero)[1].at[columns].set(portions[1])
    qkv = running.astype(jnp.bfloat16).reshape(samples, seq_len, 3, head_dim)
    query_rows = qkv[:, :, 0]
    key_matrix_rows = qkv[:, :, 1]
    value_matrix_rows = qkv[:, :, 2]
    attention_scores = jnp.einsum(
        "lph,lih->lpi", query_rows, key_matrix_rows, preferred_element_type=jnp.float32
    ) / math.sqrt(head_dim)
    attention_scores = attention_scores - jnp.max(attention_scores, axis=-1, keepdims=True)
    expo = jnp.exp(attention_scores)
    attention_probabilities = (expo / jnp.sum(expo, axis=-1, keepdims=True)).astype(jnp.bfloat16)
    attended = jnp.einsum(
        "ftn,fnv->ftv",
        attention_probabilities,
        value_matrix_rows,
        preferred_element_type=jnp.float32,
    ).astype(jnp.bfloat16)
    attended_flat = attended.reshape(samples * seq_len, head_dim)
    projected = lax.dot_general(
        attended_flat, positioned, (((1,), (1,)), ((), ())), preferred_element_type=jnp.float32
    )
    ordered = projected.reshape(samples, seq_len, model_width)
    head_term = ordered.astype(jnp.bfloat16)
    proj = lax.psum_scatter(head_term, "tensor", scatter_dimension=1, tiled=True).astype(
        jnp.float32
    )
    hidden = latent_f + gate_rows * proj
    time_float = timestep.astype(jnp.float32)
    step_size = ((time_float + 1.0) / step_count)[:, None, None]
    mean = latent_f - step_size * hidden
    noise_sigma_scale = 0.3 + 0.1 * time_float
    residual = stored_sample.astype(jnp.float32) - mean
    partial_sums = jnp.sum(residual * residual, axis=(1, 2))
    totals = lax.psum(partial_sums, "tensor")
    log_prob = (
        -totals / (2.0 * noise_sigma_scale * noise_sigma_scale * seq_len * model_width)
        - jnp.log(noise_sigma_scale)
        - 0.5 * math.log(2.0 * math.pi)
    )
    return (mean.astype(jnp.bfloat16), log_prob)


def solution(mesh):
    in_specs = (
        P("group", "tensor", None),
        P("group", "tensor", None),
        P("group"),
        P(),
        P(),
        P("group", "tensor"),
        P("tensor", "group"),
    )
    out_specs = (P("group", "tensor", None), P("group"))
    return jax.shard_map(shards, mesh=mesh, in_specs=in_specs, out_specs=out_specs, check_vma=False)
```

profile of v0, /device:TPU:0, one launch (start us, length us, event | category | flops | bytes accessed | tf_op | source)
XLA Modules:
  0.0 146.0 jit_solution(7050774255372192272)
XLA Ops:
  7.2 0.0 copy-start
  7.2 0.0 copy-start.3
  7.2 0.0 all-gather.3.cloned.1.call-start
  7.9 0.2 copy-done
  8.1 0.3 fusion.29
  8.4 1.1 convert_reduce_fusion
  9.6 1.3 fusion.9
  10.9 2.0 %fusion.12 = bf16[1,64,3072]{2,1,0:T(8,128)(2,1)} fusion(bf16[1,64,3072]{2,1,0:T(8,128)(2,1)} %param.7, f32[3072]{0:T(1024)S(1)} %bitcast.65, f32[3072]{0:T(1024)S(1)} %bitcast.64, f32[64]{0:T(128)S(1)} %add_rsqrt_fusion, f32[64]{0:T(128)S(1)} %broadcast_multiply_fusion), kind=kLoop, calls=%fused_computation.19 | loop fusion | flops 1179648 | bytes 811520 | tf_op jit(solution)/shard_map/convert_element_type | solution.py:28
  12.8 0.0 copy-start.4
  12.8 0.0 all-gather.3.cloned.1.call-update
  12.9 0.0 all-gather.5.cloned.1.call-start
  12.9 0.7 all-gather.5.cloned.1.call-update
  13.6 0.0 reduce-scatter.2.cloned.1.call-start
  13.7 0.0 copy-done.3
  13.7 12.4 %all_gather.11 = bf16[3072,128]{0,1:T(8,128)(2,1)S(1)} all-gather(bf16[384,128]{0,1:T(8,128)(2,1)S(1)} %bitcast.58), channel_id=1, replica_groups=mesh['group'=8,'tensor'=4] {'group'}, dimensions={0}, use_global_device_ids=true | all-gather | bytes 884736 | tf_op jit(solution)/shard_map/all_gather | solution.py:38
  26.1 0.4 copy.22
  26.4 0.1 compare_reduce_fusion
  26.5 0.0 copy-done.4
  26.5 0.1 select_reduce_fusion
  26.7 0.7 fusion.36
  27.3 4.4 %compare_select_fusion.2 = s32[3072,1]{0,1:T(1,128)S(1)} fusion(s32[]{:T(128)} %bitcast.6, s32[]{:T(128)} %bitcast.7, s32[]{:T(128)} %bitcast.8, s32[]{:T(128)} %bitcast.9, s32[]{:T(128)} %bitcast.10, s32[]{:T(128)} %bitcast.12, s32[]{:T(128)} %bitcast.11), kind=kLoop, calls=%fused_computation.37 | loop fusion | flops 70656 | bytes 12316 | tf_op jit(solution)/shard_map/gather | solution.py:41
  31.7 0.7 compare_and_fusion
  32.4 0.1 compare_select_fusion
  32.5 8.5 %scatter_custom_fusion = bf16[3072,128]{1,0:T(8,128)(2,1)S(1)} fusion(s32[3072]{0:T(1024)S(1)} %bitcast.60, bf16[3072,128]{1,0:T(8,128)(2,1)S(1)} %copy.22, bf16[]{:T(256)} %constant.70.clone.1), kind=kCustom, calls=%fused_computation.24 | custom fusion | bytes 786434 | tf_op jit(solution)/shard_map/scatter | solution.py:44
  41.0 11.8 %all-gather.3.cloned.1.call-done = bf16[1,256,3072]{2,1,0:T(8,128)(2,1)} async-done(((bf16[1,64,3072]{2,1,0:T(8,128)(2,1)}), bf16[1,256,3072]{2,1,0:T(8,128)(2,1)}) %all-gather.3.cloned.1.call-update) | async-done | bytes 1572880 | tf_op jit(solution)/shard_map/all_gather | solution.py:29
  52.8 1.7 %copy.17 = bf16[256,3072]{0,1:T(8,128)(2,1)S(1)} copy(bf16[256,3072]{1,0:T(8,128)(2,1)} %bitcast.55) | data formatting | bytes 3145728 | tf_op jit(solution)/shard_map/reshape | solution.py:30
  54.5 12.9 %gather_fusion = bf16[3072,256]{1,0:T(8,128)(2,1)} fusion(bf16[256,3072]{0,1:T(8,128)(2,1)S(1)} %copy.17, s32[3072]{0:T(1024)S(1)} %broadcast_clamp_fusion), kind=kCustom, calls=%fused_computation | custom fusion | bytes 3158016 | tf_op jit(solution)/shard_map/jit(_take)/gather | solution.py:42
  67.5 15.1 %all-gather.5.cloned.1.call-done = bf16[3072,384]{1,0:T(8,128)(2,1)} async-done(((bf16[384,384]{1,0:T(8,128)(2,1)}), bf16[3072,384]{1,0:T(8,128)(2,1)}) %all-gather.5.cloned.1.call-update) | async-done | bytes 2359312 | tf_op jit(solution)/shard_map/all_gather | solution.py:37
  82.6 4.1 %fusion.4 = bf16[256,384]{1,0:T(8,128)(2,1)S(1)} fusion(bf16[3072,384]{1,0:T(8,128)(2,1)} %all-gather.5.cloned.1.call-done, bf16[3072,256]{1,0:T(8,128)(2,1)} %gather_fusion, pred[3072]{0:T(1024)(128)(4,1)S(1)} %get-tuple-element.2), kind=kOutput, calls=%fused_computation.11 | convolution fusion | flops 604864512 | bytes 4131840 | tf_op jit(solution)/shard_map/dot_general | solution.py:43
  86.7 0.1 copy.18
  86.9 0.3 fusion.37
  87.1 0.1 fusion.18
  87.2 0.0 copy-start.1
  87.2 0.0 copy-start.2
  87.2 1.9 %fusion = bf16[1,256,3072]{2,1,0:T(8,128)(2,1)} fusion(bf16[3072,128]{1,0:T(8,128)(2,1)S(1)} %scatter_custom_fusion, f32[256,256]{0,1:T(8,128)S(1)} %get-tuple-element.17, f32[256]{0:T(256)S(1)} %fusion.18, f32[256]{0:T(256)S(1)} %get-tuple-element.16, bf16[1,256,3,128]{1,3,2,0:T(8,128)(2,1)S(1)} %bitcast.57), kind=kOutput, calls=%fused_computation.3 | convolution fusion | flops 219119616 | bytes 2689024 | tf_op jit(solution)/shard_map/dot_general | solution.py:62
  89.1 0.0 reduce-scatter.2.cloned.1.call-update
  89.2 35.4 %reduce-scatter.2.cloned.1.call-done = bf16[1,64,3072]{2,1,0:T(8,128)(2,1)} async-done(((bf16[1,256,3072]{2,1,0:T(8,128)(2,1)}), bf16[1,64,3072]{2,1,0:T(8,128)(2,1)}) %reduce-scatter.2.cloned.1.call-update) | async-done | bytes 393232 | tf_op jit(solution)/shard_map/reduce_scatter | solution.py:67
  124.6 0.0 copy-done.1
  124.6 0.0 copy-done.2
  124.6 2.7 %multiply_reduce_fusion = (f32[]{:T(128)}, bf16[1,64,3072]{2,1,0:T(8,128)(2,1)}) fusion(bf16[1,64,3072]{2,1,0:T(8,128)(2,1)S(1)} %copy-done.2, bf16[1,64,3072]{2,1,0:T(8,128)(2,1)} %reduce-scatter.2.cloned.1.call-done, bf16[1,64,3072]{2,1,0:T(8,128)(2,1)S(1)} %copy-done.1, f32[3072]{0:T(1024)S(1)} %bitcast.59, f32[]{:T(128)} %bitcast), kind=kLoop, calls=%fused_computation.22 | loop fusion | flops 2162687 | bytes 1585160 | tf_op jit(solution)/shard_map/reduce_sum | solution.py:76
  127.3 10.4 %psum.7 = f32[1]{0:T(128)} all-reduce(f32[1]{0:T(128)} %bitcast.25), channel_id=1, replica_groups=mesh['group'=8,'tensor'=4] {'tensor'}, use_global_device_ids=true, to_apply=%region_8.9 | all-reduce | flops 1 | bytes 8 | tf_op jit(solution)/shard_map/psum | solution.py:77
  (5 shorter events, 0.0 us)
Async XLA Ops:
  7.2 1.0 copy-start
  7.2 6.5 %copy-start.3 = (bf16[128,384]{1,0:T(8,128)(2,1)S(1)}, bf16[128,384]{1,0:T(8,128)(2,1)}, u32[]{:S(2)}) copy-start(bf16[128,384]{1,0:T(8,128)(2,1)} %param.13) | copy-start | bytes 294916
  7.2 45.6 %all-gather.3.cloned.1.call-start = ((), (), s32[]{:S(2)}) async-start(), calls=%async_computation.1 | async-start | bytes 1966080 | tf_op jit(solution)/shard_map/all_gather | solution.py:29
  12.8 13.7 %copy-start.4 = (s32[8]{0:T(128)S(1)}, s32[8]{0:T(128)}, u32[]{:S(2)}) copy-start(s32[8]{0:T(128)} %param.10) | copy-start | bytes 100
  12.9 69.7 %all-gather.5.cloned.1.call-start = ((), (), s32[]{:S(2)}) async-start(), calls=%async_computation.2 | async-start | bytes 2654208 | tf_op jit(solution)/shard_map/all_gather | solution.py:37
  13.6 110.9 %reduce-scatter.2.cloned.1.call-start = ((), (), s32[]{:S(2)}) async-start(), calls=%async_computation.3 | async-start | bytes 1966080 | tf_op jit(solution)/shard_map/reduce_scatter | solution.py:67
  87.2 37.4 %copy-start.1 = (bf16[1,64,3072]{2,1,0:T(8,128)(2,1)S(1)}, bf16[1,64,3072]{2,1,0:T(8,128)(2,1)}, u32[]{:S(2)}) copy-start(bf16[1,64,3072]{2,1,0:T(8,128)(2,1)} %param.7) | copy-start | bytes 1179652
  87.2 37.4 %copy-start.2 = (bf16[1,64,3072]{2,1,0:T(8,128)(2,1)S(1)}, bf16[1,64,3072]{2,1,0:T(8,128)(2,1)}, u32[]{:S(2)}) copy-start(bf16[1,64,3072]{2,1,0:T(8,128)(2,1)} %param.8) | copy-start | bytes 1179652
Sparse Core Ops, SparseCore 0:
  13.0 39.7 all-gather.2
  54.7 27.8 all-gather.4
  89.2 35.2 reduce-scatter.1
where the time goes:
time: 146 us
  waiting for transfers between devices  63.1 us (43%)
  local copies, waits for them, and re-layouts  24.6 us (17%)
  blocking collectives  22.8 us (16%)
  between operations  16.5 us (11%)
  other arithmetic  12.5 us (9%)
  matrix products  6.5 us (4%)
    reduce_scatter x1, waiting for transfers between devices, shards(): lax.psum_scatter(head_term, 'tensor', scatter_dimension=1, tiled=True)  35.4 us
    all_gather x1, waiting for transfers between devices, shards(): lax.all_gather(qkv_weight, 'group', axis=0, tiled=True)  15.1 us
    gather x1, local copies, waits for them, and re-layouts, shards(): picked = jnp.take(flat_rows, columns, axis=1)  12.9 us
    all_gather x1, blocking collectives, shards(): lax.all_gather(out_rows, 'group', axis=0, tiled=True)  12.4 us
    all_gather x1, waiting for transfers between devices, shards(): gathered = lax.all_gather(modulated, 'tensor', axis=1, tiled=True)  11.8 us
    psum x1, blocking collectives, shards(): totals = lax.psum(partial_sums, 'tensor')  10.4 us
    scatter x1, local copies, waits for them, and re-layouts, shards(): positioned = (qkv_zero, placed_zero)[1].at[columns].set(portions[1])  8.52 us
    gather x2, other arithmetic, shards(): slot_of[row_index // slice_rows] * slice_rows + row_index % slice_rows  4.49 us
  transfers between devices with their start and end apart: 3, of which 3 were waited for; matrix products, arithmetic and copies ran while one was open for 20% of the time, Pallas kernels for 0%

commit v1 on v0

--- a/solution.py
+++ b/solution.py
@@ -1,9 +1,386 @@
+import functools
 import math
 
 import jax
 import jax.numpy as jnp
 from jax import lax
+from jax.experimental import pallas as pl
+from jax.experimental.pallas import tpu as pltpu
 from jax.sharding import PartitionSpec as P
+
+MESH = pl.DeviceIdType.MESH
+F32 = jnp.float32
+BF16 = jnp.bfloat16
+
+
+def fused_kernel(
+    groups,
+    cycle,
+    step_count,
+    owner_ref,
+    step_ref,
+    lat_hbm,
+    sto_hbm,
+    mod_hbm,
+    wq_hbm,
+    wo_hbm,
+    out_ref,
+    logp_ref,
+    lat,
+    sto,
+    mod,
+    wq,
+    wo,
+    xg,
+    qkv,
+    att,
+    attg,
+    part,
+    local_sem,
+    ws,
+    wr,
+    zs,
+    zr,
+    xs,
+    xr,
+    as_,
+    ar,
+    ps,
+    pr,
+):
+    g = lax.axis_index("group")
+    t = lax.axis_index("tensor")
+    slices, tok, width = xg.shape[1:]
+    head_dim = wo.shape[2]
+    chunks = xr.shape[1]
+    per_chunk = slices // chunks
+    bits = [1 << i for i in range(1, groups.bit_length() - 1)]
+    masks = sorted(range(0, groups, 2), key=lambda m: bin(m).count("1"))
+    orders = (bits, bits[::-1])
+
+    barrier = pltpu.get_barrier_semaphore()
+    partners = [dict(group=g ^ b, tensor=t) for b in [1] + bits]
+    partners += [dict(group=g, tensor=lax.rem(t + k, cycle)) for k in range(1, cycle)]
+    for who in partners:
+        pl.semaphore_signal(
+            barrier, inc=1, device_id=(who["group"], who["tensor"]), device_id_type=MESH
+        )
+    locals_ = [
+        pltpu.make_async_copy(lat_hbm.at[0], lat, local_sem.at[0]),
+        pltpu.make_async_copy(mod_hbm, mod, local_sem.at[1]),
+        pltpu.make_async_copy(wq_hbm, wq.at[g], local_sem.at[2]),
+        pltpu.make_async_copy(wo_hbm, wo.at[g, t], local_sem.at[3]),
+        pltpu.make_async_copy(sto_hbm.at[0], sto, local_sem.at[4]),
+    ]
+    for copy in locals_:
+        copy.start()
+    pl.semaphore_wait(barrier, len(partners))
+
+    def piece(payload, head, src_group, half):
+        if payload is None:
+            rows = wq.shape[1] // 2
+            return wq.at[src_group, pl.ds(half * rows, rows)]
+        rows = head_dim // 2
+        return wo.at[src_group, head, pl.ds(half * rows, rows)]
+
+    def plane_copy(head, mask, half, lane, src=None):
+        index = 0 if head is None else 1 + head
+        origin = g ^ mask
+        here = piece(None if head is None else 1, head, origin, half)
+        to = g ^ (1 if lane == 0 else bits[lane - 1])
+        return pltpu.make_async_remote_copy(
+            src_ref=here if src is None else src,
+            dst_ref=here,
+            send_sem=ws.at[index, mask >> 1, half, lane],
+            recv_sem=wr.at[index, origin, half],
+            device_id=(to, t),
+            device_id_type=MESH,
+        )
+
+    def lanes_of(mask, half):
+        order = orders[half]
+        last = max([i for i, b in enumerate(order) if mask & b], default=-1)
+        return [bits.index(b) + 1 for b in order[last + 1 :]] + [0]
+
+    def plane_send(head, mask, src_of=None):
+        for half in (0, 1):
+            for lane in lanes_of(mask, half):
+                plane_copy(head, mask, half, lane, src_of and src_of(half)).start()
+
+    def plane_wait(head, mask, half):
+        plane_copy(head, mask, half, 0).wait_recv()
+
+    def plane_relay(head, mask):
+        for half in (0, 1):
+            plane_wait(head, mask, half)
+            for lane in lanes_of(mask, half):
+                plane_copy(head, mask, half, lane).start()
+
+    def plane_partner(head):
+        for mask in masks:
+            for half in (0, 1):
+                plane_wait(head, mask | 1, half)
+
+    def plane_drain(head):
+        for mask in masks:
+            for half in (0, 1):
+                for lane in lanes_of(mask, half):
+                    plane_copy(head, mask, half, lane).wait_send()
+
+    def each_side(k, body):
+        @pl.when(t - k >= 0)
+        def _():
+            body(t - k, 0)
+
+        @pl.when(t + k < cycle)
+        def _():
+            body(t + k, 1)
+
+    def onward(direction, body):
+        if direction == 0:
+            pl.when(t + 1 < cycle)(lambda: body(t + 1))
+        else:
+            pl.when(t - 1 >= 0)(lambda: body(t - 1))
+
+    def head_copy(source, direction, k, to, src=None):
+        here = wo.at[g, source]
+        return pltpu.make_async_remote_copy(
+            src_ref=here if src is None else src,
+            dst_ref=here,
+            send_sem=zs.at[direction, k],
+            recv_sem=zr.at[source],
+            device_id=(g, to),
+            device_id_type=MESH,
+        )
+
+    def token_copy(source, direction, k, c, to):
+        here = xg.at[source, pl.ds(c * per_chunk, per_chunk)]
+        return pltpu.make_async_remote_copy(
+            src_ref=here,
+            dst_ref=here,
+            send_sem=xs.at[direction, k, c],
+            recv_sem=xr.at[source, c],
+            device_id=(g, to),
+            device_id_type=MESH,
+        )
+
+    half_q = wq.shape[1] // 2
+    half_o = head_dim // 2
+    for direction in (0, 1):
+        onward(direction, lambda to, d=direction: head_copy(t, d, 0, to, wo_hbm).start())
+    plane_send(None, 0, lambda half: wq_hbm.at[pl.ds(half * half_q, half_q)])
+    plane_send(t, 0, lambda half: wo_hbm.at[pl.ds(half * half_o, half_o)])
+
+    time_index = step_ref[0]
+    locals_[0].wait()
+    x = lat[...].astype(F32)
+    mean_x = jnp.mean(x, axis=-1, keepdims=True)
+    centred_x = x - mean_x
+    inv_std = lax.rsqrt(jnp.mean(centred_x * centred_x, axis=-1, keepdims=True) + 1e-06)
+    locals_[1].wait()
+    for c in range(chunks):
+        for o in range(c * per_chunk, (c + 1) * per_chunk):
+            cols = pl.ds(o * width, width)
+            piece_x = lat[:, cols].astype(F32)
+            scale = mod[time_index, pl.ds(1, 1), cols]
+            shift = mod[time_index, pl.ds(0, 1), cols]
+            normed = (piece_x - mean_x) * inv_std
+            xg[t, o] = (normed * (1.0 + scale) + shift).astype(BF16)
+        for direction in (0, 1):
+            onward(direction, lambda to, d=direction, c=c: token_copy(t, d, 0, c, to).start())
+
+    def head_step(k):
+        def body(source, direction):
+            head_copy(source, direction, k, t).wait_recv()
+            if k < cycle - 1:
+                onward(direction, lambda to: head_copy(source, direction, k, to).start())
+            plane_send(source, 0)
+
+        each_side(k, body)
+
+    def token_step(k):
+        def body(source, direction):
+            for c in range(chunks):
+                token_copy(source, direction, k, c, t).wait_recv()
+                if k < cycle - 1:
+                    onward(
+                        direction, lambda to, c=c: token_copy(source, direction, k, c, to).start()
+                    )
+
+        each_side(k, body)
+
+    def project(source):
+        acc = jnp.zeros((tok, wq.shape[2]), F32)
+        for s in range(slices):
+            acc += jnp.dot(xg[source, s], wq[owner_ref[s]], preferred_element_type=F32)
+        qkv[pl.ds(pl.multiple_of(source * tok, tok), tok), :] = acc.astype(BF16)
+
+    def relay_all(head):
+        for mask in masks[1:]:
+            plane_relay(head, mask)
+
+    head_step(1)
+    relay_all(None)
+    for k in range(2, cycle):
+        head_step(k)
+    relay_all(t)
+    token_step(1)
+    each_side(1, lambda source, d: relay_all(source))
+    locals_[2].wait()
+    locals_[3].wait()
+    plane_partner(None)
+    project(t)
+    each_side(1, lambda source, d: project(source))
+    for k in range(2, cycle):
+        token_step(k)
+        each_side(k, lambda source, d: relay_all(source))
+        each_side(k, lambda source, d: project(source))
+
+    query = qkv[:, :head_dim]
+    key = qkv[:, head_dim : 2 * head_dim]
+    value = qkv[:, 2 * head_dim :]
+    scores = lax.dot_general(
+        query, key, (((1,), (1,)), ((), ())), preferred_element_type=F32
+    ) / math.sqrt(head_dim)
+    expo = jnp.exp(scores - jnp.max(scores, axis=-1, keepdims=True))
+    probs = (expo / jnp.sum(expo, axis=-1, keepdims=True)).astype(BF16)
+    att[...] = jnp.dot(probs, value, preferred_element_type=F32).astype(BF16)
+
+    def att_copy(k):
+        to = lax.rem(t + k, cycle)
+        return pltpu.make_async_remote_copy(
+            src_ref=att.at[pl.ds(pl.multiple_of(to * tok, tok), tok)],
+            dst_ref=attg.at[t],
+            send_sem=as_.at[k],
+            recv_sem=ar.at[k],
+            device_id=(g, to),
+            device_id_type=MESH,
+        )
+
+    for k in range(1, cycle):
+        att_copy(k).start()
+    attg[t] = att[pl.ds(pl.multiple_of(t * tok, tok), tok), :]
+    for head in range(cycle):
+        plane_partner(head)
+    locals_[4].wait()
+    for k in range(1, cycle):
+        att_copy(k).wait_recv()
+    rows = jnp.concatenate([attg[h] for h in range(cycle)], axis=1)
+    time_float = time_index.astype(F32)
+    step_size = (time_float + 1.0) / step_count
+    squares = jnp.zeros((tok, width), F32)
+    for s in range(slices):
+        cols = pl.ds(s * width, width)
+        block = wo[owner_ref[s]].reshape(cycle * head_dim, width)
+        proj = jnp.dot(rows, block, preferred_element_type=F32)
+        latent = lat[:, cols].astype(F32)
+        hidden = latent + mod[time_index, pl.ds(2, 1), cols] * proj
+        mean = latent - step_size * hidden
+        out_ref[0, :, cols] = mean.astype(BF16)
+        residual = sto[:, cols].astype(F32) - mean
+        squares += residual * residual
+    folded = squares.reshape(tok // 8, 8, width).sum(axis=0)
+    part[t] = functools.reduce(
+        lambda a, b: a + b, [folded[:, i : i + 128] for i in range(0, width, 128)]
+    )
+
+    def part_copy(k):
+        return pltpu.make_async_remote_copy(
+            src_ref=part.at[t],
+            dst_ref=part.at[t],
+            send_sem=ps.at[k],
+            recv_sem=pr.at[k],
+            device_id=(g, lax.rem(t + k, cycle)),
+            device_id_type=MESH,
+        )
+
+    for k in range(1, cycle):
+        part_copy(k).start()
+    plane_drain(None)
+    for head in range(cycle):
+        plane_drain(head)
+    for direction in (0, 1):
+        onward(direction, lambda to, d=direction: head_copy(t, d, 0, to, wo_hbm).wait_send())
+        for c in range(chunks):
+            onward(direction, lambda to, d=direction, c=c: token_copy(t, d, 0, c, to).wait_send())
+
+    def drain(k):
+        def body(source, direction):
+            def sent(to):
+                head_copy(source, direction, k, to).wait_send()
+                for c in range(chunks):
+                    token_copy(source, direction, k, c, to).wait_send()
+
+            onward(direction, sent)
+
+        each_side(k, body)
+
+    for k in range(1, cycle - 1):
+        drain(k)
+    for k in range(1, cycle):
+        att_copy(k).wait_send()
+    for k in range(1, cycle):
+        part_copy(k).wait_recv()
+    total = functools.reduce(lambda a, b: a + b, [part[h] for h in range(cycle)])
+    total = jnp.sum(jnp.sum(total, axis=0, keepdims=True), axis=1, keepdims=True)
+    total = jnp.broadcast_to(total, logp_ref.shape)
+    sigma = 0.3 + 0.1 * jnp.full(logp_ref.shape, time_float, F32)
+    count = tok * cycle * slices * width
+    logp_ref[...] = (
+        -total / (2.0 * sigma * sigma * count) - jnp.log(sigma) - 0.5 * math.log(2.0 * math.pi)
+    )
+    for k in range(1, cycle):
+        part_copy(k).wait_send()
+
+
+def fused(latents, stored_sample, timestep, owner_map, mod_table, qkv_weight, out_weight):
+    groups = lax.axis_size("group")
+    cycle = lax.axis_size("tensor")
+    _, tok, model = latents.shape
+    slice_rows, columns = qkv_weight.shape
+    head_dim = out_weight.shape[0]
+    chunks = math.gcd(groups, 4)
+    lanes = groups.bit_length() - 1
+    dma = pltpu.SemaphoreType.DMA
+    smem = pl.BlockSpec(memory_space=pltpu.SMEM)
+    anyspace = pl.BlockSpec(memory_space=pl.ANY)
+    vmem = pl.BlockSpec(memory_space=pltpu.VMEM)
+    mean_next, logp = pl.pallas_call(
+        functools.partial(fused_kernel, groups, cycle, mod_table.shape[0]),
+        out_shape=(
+            jax.ShapeDtypeStruct((1, tok, model), BF16),
+            jax.ShapeDtypeStruct((8, 128), F32),
+        ),
+        in_specs=[smem, smem] + [anyspace] * 5,
+        out_specs=(vmem, vmem),
+        scratch_shapes=[
+            pltpu.VMEM((tok, model), BF16),
+            pltpu.VMEM((tok, model), BF16),
+            pltpu.VMEM(mod_table.shape, F32),
+            pltpu.VMEM((groups, slice_rows, columns), BF16),
+            pltpu.VMEM((groups, cycle, head_dim, slice_rows), BF16),
+            pltpu.VMEM((cycle, groups, tok, slice_rows), BF16),
+            pltpu.VMEM((tok * cycle, columns), BF16),
+            pltpu.VMEM((tok * cycle, head_dim), BF16),
+            pltpu.VMEM((cycle, tok, head_dim), BF16),
+            pltpu.VMEM((cycle, 8, 128), F32),
+            dma((5,)),
+            dma((1 + cycle, groups // 2, 2, lanes)),
+            dma((1 + cycle, groups, 2)),
+            dma((2, cycle)),
+            dma((cycle,)),
+            dma((2, cycle, chunks)),
+            dma((cycle, chunks)),
+            dma((cycle,)),
+            dma((cycle,)),
+            dma((cycle,)),
+            dma((cycle,)),
+        ],
+        compiler_params=pltpu.CompilerParams(
+            collective_id=0, has_side_effects=True, vmem_limit_bytes=40 * 1024 * 1024
+        ),
+    )(owner_map, timestep, latents, stored_sample, mod_table, qkv_weight, out_weight)
+    return mean_next, logp[0, :1]
 
 
 def shards(latents, stored_sample, timestep, owner_map, mod_table, qkv_weight, out_weight):
@@ -94,4 +471,23 @@
         P("tensor", "group"),
     )
     out_specs = (P("group", "tensor", None), P("group"))
-    return jax.shard_map(shards, mesh=mesh, in_specs=in_specs, out_specs=out_specs, check_vma=False)
+    groups, cycle = mesh.shape["group"], mesh.shape["tensor"]
+
+    def step(latents, stored_sample, timestep, owner_map, mod_table, qkv_weight, out_weight):
+        samples, seq_len, model = latents.shape
+        width, tok = model // groups, seq_len // cycle
+        head_dim = out_weight.shape[0] // cycle
+        fits = (
+            samples == groups
+            and groups & (groups - 1) == 0
+            and width % 128 == 0
+            and head_dim % 128 == 0
+            and tok % 16 == 0
+        )
+        args = (latents, stored_sample, timestep, owner_map, mod_table, qkv_weight, out_weight)
+        body = fused if fits else shards
+        return jax.shard_map(
+            body, mesh=mesh, in_specs=in_specs, out_specs=out_specs, check_vma=False
+        )(*args)
+
+    return step

time: 146 us -> 65.4 us (0.45)
  waiting for transfers between devices: 63.1 us -> 0 us
  Pallas kernels: 0 us -> 59.4 us
  blocking collectives: 22.8 us -> 0 us
  local copies, waits for them, and re-layouts: 24.6 us -> 4.36 us
  between operations: 16.5 us -> 1.4 us
  other arithmetic: 12.5 us -> 0 us
  matrix products: 6.5 us -> 0 us
    pallas_call x0 -> x1, Pallas kernels: none -> 59.4 us  [fused(): pl.pallas_call(functools.partial(fused_kernel, groups, cycle, mod_table.s...]
    reduce_scatter x1 -> x0, waiting for transfers between devices: 35.4 us -> none  [shards(): lax.psum_scatter(head_term, 'tensor', scatter_dimension=1, tiled=True)]
    all_gather x2 -> x0, waiting for transfers between devices: 27 us -> none  [the longest x1 15.1 us: shards(): lax.all_gather(qkv_weight, 'group', axis=0, tiled=True)]
    gather x2 -> x0, local copies, waits for them, and re-layouts: 13.6 us -> none  [the longest x1 12.9 us: shards(): picked = jnp.take(flat_rows, columns, axis=1)]
    all_gather x1 -> x0, blocking collectives: 12.4 us -> none  [shards(): lax.all_gather(out_rows, 'group', axis=0, tiled=True)]
    psum x1 -> x0, blocking collectives: 10.4 us -> none  [shards(): totals = lax.psum(partial_sums, 'tensor')]
    scatter x1 -> x0, local copies, waits for them, and re-layouts: 8.52 us -> none  [shards(): positioned = (qkv_zero, placed_zero)[1].at[columns].set(portions[1])]
    dot_general x4 -> x0, matrix products: 6.5 us -> none  [the longest x1 4.1 us: shards(): running = jnp.dot(picked, portions[0], preferred_element_type=jnp.float32)]
  transfers between devices with their start and end apart: 3 -> 0, of which waited for: 3 -> 0; matrix products, arithmetic and copies ran while one was open for 20% -> 0% of each run, Pallas kernels for 0% -> 0%
where the time goes in v1:
time: 65.4 us; the launch traced here: 65.2 us
  Pallas kernels  59.4 us (91%)
  local copies, waits for them, and re-layouts  4.36 us (7%)
  between operations  1.4 us (2%)
    pallas_call x1, Pallas kernels, fused(): pl.pallas_call(functools.partial(fused_kernel, groups, cycle, mod_table.s...  59.4 us
    unnamed x12, local copies, waits for them, and re-layouts  3.85 us

profile of v1, /device:TPU:0, one launch (start us, length us, event | category | flops | bytes accessed | tf_op | source)
XLA Modules:
  0.0 65.2 jit_solution(7997909655074340118)
XLA Ops:
  0.6 0.0 copy-start
  1.3 0.0 copy-start.2
  1.3 0.0 copy-start.4
  1.4 1.2 %copy.9.mod_hbm = f32[8,3,3072]{2,1,0:T(4,128)S(1)} copy(f32[8,3,3072]{2,0,1:T(8,128)} %param.11) | data formatting | bytes 589824 | tf_op args[4]
  2.6 0.0 copy-done
  2.6 0.0 copy-done.2
  2.6 0.0 copy-done.4
  2.6 0.0 copy-start.1
  2.6 1.0 %copy-done.1 = bf16[1,64,3072]{2,1,0:T(8,128)(2,1)S(1)} copy-done((bf16[1,64,3072]{2,1,0:T(8,128)(2,1)S(1)}, bf16[1,64,3072]{2,1,0:T(8,128)(2,1)}, u32[]{:S(2)}) %copy-start.1) | copy-done | bytes 393240
  3.6 0.0 copy-start.3
  3.6 0.9 %copy-done.3 = bf16[128,384]{1,0:T(8,128)(2,1)S(1)} copy-done((bf16[128,384]{1,0:T(8,128)(2,1)S(1)}, bf16[128,384]{1,0:T(8,128)(2,1)}, u32[]{:S(2)}) %copy-start.3) | copy-done | bytes 98328
  4.5 59.4 %shard_map.86 = (bf16[1,64,3072]{2,1,0:T(8,128)(2,1)S(1)}, f32[8,128]{1,0:T(8,128)S(1)}) custom-call(s32[8]{0:T(128)S(1)} %copy-done.4, s32[1]{0:T(128)S(6)} %copy.11.step_ref, bf16[1,64,3072]{2,1,0:T(8,128)(2,1)S(1)} %copy-done, bf16[1,64,3072]{2,1,0:T(8,128)(2,1)S(1)} %copy-done.1, f32[8,3,3072]{2,1,0:T(4,128)S(1)} %copy.9.mod_hbm, ...), custom_call_target="tpu_custom_call" | custom-call | tf_op jit(solution)/shard_map/pallas_call | solution.py:348
  63.9 0.5 slice.3
  64.4 0.7 %copy.12 = bf16[1,64,3072]{2,1,0:T(8,128)(2,1)} copy(bf16[1,64,3072]{2,1,0:T(8,128)(2,1)S(1)} %get-tuple-element.8) | data formatting | bytes 786432
Async XLA Ops:
  0.6 1.9 %copy-start = (bf16[1,64,3072]{2,1,0:T(8,128)(2,1)S(1)}, bf16[1,64,3072]{2,1,0:T(8,128)(2,1)}, u32[]{:S(2)}) copy-start(bf16[1,64,3072]{2,1,0:T(8,128)(2,1)} %lat_hbm.1) | copy-start | bytes 1179652
  1.3 1.2 %copy-start.2 = (bf16[384,384]{1,0:T(8,128)(2,1)S(1)}, bf16[384,384]{1,0:T(8,128)(2,1)}, u32[]{:S(2)}) copy-start(bf16[384,384]{1,0:T(8,128)(2,1)} %wq_hbm.1) | copy-start | bytes 884740
  1.3 1.2 %copy-start.4 = (s32[8]{0:T(128)S(1)}, s32[8]{0:T(128)}, u32[]{:S(2)}) copy-start(s32[8]{0:T(128)} %owner_ref.1) | copy-start | bytes 100
  2.6 1.0 %copy-start.1 = (bf16[1,64,3072]{2,1,0:T(8,128)(2,1)S(1)}, bf16[1,64,3072]{2,1,0:T(8,128)(2,1)}, u32[]{:S(2)}) copy-start(bf16[1,64,3072]{2,1,0:T(8,128)(2,1)} %sto_hbm.1) | copy-start | bytes 1179652
  3.6 0.9 %copy-start.3 = (bf16[128,384]{1,0:T(8,128)(2,1)S(1)}, bf16[128,384]{1,0:T(8,128)(2,1)}, u32[]{:S(2)}) copy-start(bf16[128,384]{1,0:T(8,128)(2,1)} %wo_hbm.1) | copy-start | bytes 294916

commit v2 on v1

--- a/solution.py
+++ b/solution.py
@@ -110,12 +110,6 @@
     def plane_wait(head, mask, half):
         plane_copy(head, mask, half, 0).wait_recv()
 
-    def plane_relay(head, mask):
-        for half in (0, 1):
-            plane_wait(head, mask, half)
-            for lane in lanes_of(mask, half):
-                plane_copy(head, mask, half, lane).start()
-
     def plane_partner(head):
         for mask in masks:
             for half in (0, 1):
@@ -142,14 +136,14 @@
         else:
             pl.when(t - 1 >= 0)(lambda: body(t - 1))
 
-    def head_copy(source, direction, k, to, src=None):
-        here = wo.at[g, source]
+    def head_copy(k):
+        here = wo.at[g, t]
         return pltpu.make_async_remote_copy(
-            src_ref=here if src is None else src,
+            src_ref=wo_hbm,
             dst_ref=here,
-            send_sem=zs.at[direction, k],
-            recv_sem=zr.at[source],
-            device_id=(g, to),
+            send_sem=zs.at[k],
+            recv_sem=zr.at[k],
+            device_id=(g, lax.rem(t + k, cycle)),
             device_id_type=MESH,
         )
 
@@ -166,8 +160,8 @@
 
     half_q = wq.shape[1] // 2
     half_o = head_dim // 2
-    for direction in (0, 1):
-        onward(direction, lambda to, d=direction: head_copy(t, d, 0, to, wo_hbm).start())
+    for k in range(1, cycle):
+        head_copy(k).start()
     plane_send(None, 0, lambda half: wq_hbm.at[pl.ds(half * half_q, half_q)])
     plane_send(t, 0, lambda half: wo_hbm.at[pl.ds(half * half_o, half_o)])
 
@@ -182,59 +176,67 @@
         for o in range(c * per_chunk, (c + 1) * per_chunk):
             cols = pl.ds(o * width, width)
             piece_x = lat[:, cols].astype(F32)
-            scale = mod[time_index, pl.ds(1, 1), cols]
-            shift = mod[time_index, pl.ds(0, 1), cols]
+            scale = mod[1, pl.ds(time_index, 1), cols]
+            shift = mod[0, pl.ds(time_index, 1), cols]
             normed = (piece_x - mean_x) * inv_std
             xg[t, o] = (normed * (1.0 + scale) + shift).astype(BF16)
         for direction in (0, 1):
             onward(direction, lambda to, d=direction, c=c: token_copy(t, d, 0, c, to).start())
 
     def head_step(k):
+        head_copy(k).wait_recv()
+        plane_send(lax.rem(t - k + cycle, cycle), 0)
+
+    def token_step(k, c):
         def body(source, direction):
-            head_copy(source, direction, k, t).wait_recv()
+            token_copy(source, direction, k, c, t).wait_recv()
             if k < cycle - 1:
-                onward(direction, lambda to: head_copy(source, direction, k, to).start())
-            plane_send(source, 0)
+                onward(direction, lambda to: token_copy(source, direction, k, c, to).start())
 
         each_side(k, body)
 
-    def token_step(k):
-        def body(source, direction):
-            for c in range(chunks):
-                token_copy(source, direction, k, c, t).wait_recv()
-                if k < cycle - 1:
-                    onward(
-                        direction, lambda to, c=c: token_copy(source, direction, k, c, to).start()
-                    )
-
-        each_side(k, body)
-
-    def project(source):
+    def relay(k, mask, half):
+        head = None if k is None else lax.rem(t - k + cycle, cycle)
+        plane_wait(head, mask, half)
+        for lane in lanes_of(mask, half):
+            plane_copy(head, mask, half, lane).start()
+
+    def project(source, wait=None):
         acc = jnp.zeros((tok, wq.shape[2]), F32)
         for s in range(slices):
+            if wait is not None and s % per_chunk == 0:
+                wait(s // per_chunk)
             acc += jnp.dot(xg[source, s], wq[owner_ref[s]], preferred_element_type=F32)
         qkv[pl.ds(pl.multiple_of(source * tok, tok), tok), :] = acc.astype(BF16)
 
-    def relay_all(head):
-        for mask in masks[1:]:
-            plane_relay(head, mask)
-
-    head_step(1)
-    relay_all(None)
-    for k in range(2, cycle):
-        head_step(k)
-    relay_all(t)
-    token_step(1)
-    each_side(1, lambda source, d: relay_all(source))
+    events = []
+    for k in range(1, cycle):
+        events.append((2 + 2 * k, functools.partial(head_step, k)))
+    for k in range(1, cycle - 1):
+        for c in range(chunks):
+            events.append((6 + 8 * (k - 1 + c / chunks), functools.partial(token_step, k, c)))
+    for mask in masks[1:]:
+        far = bin(mask).count("1") - 1
+        for half in (0, 1):
+            events.append((5 + 2 * half + 6 * far, functools.partial(relay, None, mask, half)))
+            for k in range(cycle):
+                at = 9 + 3 * k + half + 7 * far
+                events.append((at, functools.partial(relay, k, mask, half)))
+    for _, event in sorted(events, key=lambda e: e[0]):
+        event()
     locals_[2].wait()
     locals_[3].wait()
     plane_partner(None)
     project(t)
-    each_side(1, lambda source, d: project(source))
-    for k in range(2, cycle):
-        token_step(k)
-        each_side(k, lambda source, d: relay_all(source))
+    for k in range(1, cycle - 1):
         each_side(k, lambda source, d: project(source))
+    last = cycle - 1
+    each_side(
+        last,
+        lambda source, d: project(
+            source, lambda c: token_copy(source, d, last, c, t).wait_recv()
+        ),
+    )
 
     query = qkv[:, :head_dim]
     key = qkv[:, head_dim : 2 * head_dim]
@@ -274,7 +276,7 @@
         block = wo[owner_ref[s]].reshape(cycle * head_dim, width)
         proj = jnp.dot(rows, block, preferred_element_type=F32)
         latent = lat[:, cols].astype(F32)
-        hidden = latent + mod[time_index, pl.ds(2, 1), cols] * proj
+        hidden = latent + mod[2, pl.ds(time_index, 1), cols] * proj
         mean = latent - step_size * hidden
         out_ref[0, :, cols] = mean.astype(BF16)
         residual = sto[:, cols].astype(F32) - mean
@@ -300,14 +302,12 @@
     for head in range(cycle):
         plane_drain(head)
     for direction in (0, 1):
-        onward(direction, lambda to, d=direction: head_copy(t, d, 0, to, wo_hbm).wait_send())
         for c in range(chunks):
             onward(direction, lambda to, d=direction, c=c: token_copy(t, d, 0, c, to).wait_send())
 
     def drain(k):
         def body(source, direction):
             def sent(to):
-                head_copy(source, direction, k, to).wait_send()
                 for c in range(chunks):
                     token_copy(source, direction, k, c, to).wait_send()
 
@@ -318,17 +318,18 @@
     for k in range(1, cycle - 1):
         drain(k)
     for k in range(1, cycle):
+        head_copy(k).wait_send()
         att_copy(k).wait_send()
     for k in range(1, cycle):
         part_copy(k).wait_recv()
     total = functools.reduce(lambda a, b: a + b, [part[h] for h in range(cycle)])
     total = jnp.sum(jnp.sum(total, axis=0, keepdims=True), axis=1, keepdims=True)
-    total = jnp.broadcast_to(total, logp_ref.shape)
-    sigma = 0.3 + 0.1 * jnp.full(logp_ref.shape, time_float, F32)
+    sigma = 0.3 + 0.1 * jnp.full((1, 1), time_float, F32)
     count = tok * cycle * slices * width
-    logp_ref[...] = (
+    result = (
         -total / (2.0 * sigma * sigma * count) - jnp.log(sigma) - 0.5 * math.log(2.0 * math.pi)
     )
+    logp_ref[0] = jnp.sum(result)
     for k in range(1, cycle):
         part_copy(k).wait_send()
 
@@ -345,18 +346,19 @@
     smem = pl.BlockSpec(memory_space=pltpu.SMEM)
     anyspace = pl.BlockSpec(memory_space=pl.ANY)
     vmem = pl.BlockSpec(memory_space=pltpu.VMEM)
-    mean_next, logp = pl.pallas_call(
+    table = mod_table.transpose(1, 0, 2)
+    return pl.pallas_call(
         functools.partial(fused_kernel, groups, cycle, mod_table.shape[0]),
         out_shape=(
             jax.ShapeDtypeStruct((1, tok, model), BF16),
-            jax.ShapeDtypeStruct((8, 128), F32),
+            jax.ShapeDtypeStruct((1,), F32),
         ),
         in_specs=[smem, smem] + [anyspace] * 5,
-        out_specs=(vmem, vmem),
+        out_specs=(vmem, smem),
         scratch_shapes=[
             pltpu.VMEM((tok, model), BF16),
             pltpu.VMEM((tok, model), BF16),
-            pltpu.VMEM(mod_table.shape, F32),
+            pltpu.VMEM(table.shape, F32),
             pltpu.VMEM((groups, slice_rows, columns), BF16),
             pltpu.VMEM((groups, cycle, head_dim, slice_rows), BF16),
             pltpu.VMEM((cycle, groups, tok, slice_rows), BF16),
@@ -367,7 +369,7 @@
             dma((5,)),
             dma((1 + cycle, groups // 2, 2, lanes)),
             dma((1 + cycle, groups, 2)),
-            dma((2, cycle)),
+            dma((cycle,)),
             dma((cycle,)),
             dma((2, cycle, chunks)),
             dma((cycle, chunks)),
@@ -377,10 +379,9 @@
             dma((cycle,)),
         ],
         compiler_params=pltpu.CompilerParams(
-            collective_id=0, has_side_effects=True, vmem_limit_bytes=40 * 1024 * 1024
+            collective_id=0, has_side_effects=True, vmem_limit_bytes=60 * 1024 * 1024
         ),
-    )(owner_map, timestep, latents, stored_sample, mod_table, qkv_weight, out_weight)
-    return mean_next, logp[0, :1]
+    )(owner_map, timestep, latents, stored_sample, table, qkv_weight, out_weight)
 
 
 def shards(latents, stored_sample, timestep, owner_map, mod_table, qkv_weight, out_weight):

time: 65.4 us -> 56.2 us (0.86)
  Pallas kernels: 59.4 us -> 51.2 us
  local copies, waits for them, and re-layouts: 4.36 us -> 1.77 us
  between operations: 1.4 us -> 3.04 us
    pallas_call x1, Pallas kernels: 59.4 us -> 51.2 us  [fused(): pl.pallas_call(functools.partial(fused_kernel, groups, cycle, mod_table.s...]
    unnamed x12 -> x1, local copies, waits for them, and re-layouts: 3.85 us -> 1.77 us
where the time goes in v2:
time: 56.2 us; the launch traced here: 56 us
  Pallas kernels  51.2 us (91%)
  between operations  3.04 us (5%)
  local copies, waits for them, and re-layouts  1.77 us (3%)
    pallas_call x1, Pallas kernels, fused(): pl.pallas_call(functools.partial(fused_kernel, groups, cycle, mod_table.s...  51.2 us
    unnamed x1, local copies, waits for them, and re-layouts  1.77 us

profile of v2, /device:TPU:0, one launch (start us, length us, event | category | flops | bytes accessed | tf_op | source)
XLA Modules:
  0.0 56.0 jit_solution(16488156303499383340)
XLA Ops:
  1.3 51.2 %shard_map.86 = (bf16[1,64,3072]{2,1,0:T(8,128)(2,1)}, f32[1]{0:T(128)}) custom-call(s32[8]{0:T(128)} %owner_ref.1, s32[1]{0:T(128)S(6)} %copy.11.step_ref, bf16[1,64,3072]{2,1,0:T(8,128)(2,1)} %lat_hbm.1, bf16[1,64,3072]{2,1,0:T(8,128)(2,1)} %sto_hbm.1, f32[3,8,3072]{2,1,0:T(8,128)} %bitcast.1, bf16[384,384]{1,0:T(8,128)(2,1)} %wq_hbm.1, ...), custom_call_target="tpu_custom_call" | custom-call | tf_op jit(solution)/shard_map/pallas_call | solution.py:350
  52.4 1.8 %copy.12 = bf16[1,64,3072]{2,1,0:T(8,128)(2,1)} copy(bf16[1,64,3072]{2,1,0:T(8,128)(2,1)} %get-tuple-element.4) | data formatting | bytes 786432

commit v3 on v2

--- a/solution.py
+++ b/solution.py
@@ -74,6 +74,12 @@
     ]
     for copy in locals_:
         copy.start()
+    time_index = step_ref[0]
+    locals_[0].wait()
+    x = lat[...].astype(F32)
+    mean_x = jnp.mean(x, axis=-1, keepdims=True)
+    centred_x = x - mean_x
+    inv_std = lax.rsqrt(jnp.mean(centred_x * centred_x, axis=-1, keepdims=True) + 1e-06)
     pl.semaphore_wait(barrier, len(partners))
 
     def piece(payload, head, src_group, half):
@@ -165,12 +171,6 @@
     plane_send(None, 0, lambda half: wq_hbm.at[pl.ds(half * half_q, half_q)])
     plane_send(t, 0, lambda half: wo_hbm.at[pl.ds(half * half_o, half_o)])
 
-    time_index = step_ref[0]
-    locals_[0].wait()
-    x = lat[...].astype(F32)
-    mean_x = jnp.mean(x, axis=-1, keepdims=True)
-    centred_x = x - mean_x
-    inv_std = lax.rsqrt(jnp.mean(centred_x * centred_x, axis=-1, keepdims=True) + 1e-06)
     locals_[1].wait()
     for c in range(chunks):
         for o in range(c * per_chunk, (c + 1) * per_chunk):
@@ -344,7 +344,7 @@
     lanes = groups.bit_length() - 1
     dma = pltpu.SemaphoreType.DMA
     smem = pl.BlockSpec(memory_space=pltpu.SMEM)
-    anyspace = pl.BlockSpec(memory_space=pl.ANY)
+    hbm = pl.BlockSpec(memory_space=pltpu.HBM)
     vmem = pl.BlockSpec(memory_space=pltpu.VMEM)
     table = mod_table.transpose(1, 0, 2)
     return pl.pallas_call(
@@ -353,7 +353,7 @@
             jax.ShapeDtypeStruct((1, tok, model), BF16),
             jax.ShapeDtypeStruct((1,), F32),
         ),
-        in_specs=[smem, smem] + [anyspace] * 5,
+        in_specs=[smem, smem] + [hbm] * 5,
         out_specs=(vmem, smem),
         scratch_shapes=[
             pltpu.VMEM((tok, model), BF16),
@@ -379,7 +379,7 @@
             dma((cycle,)),
         ],
         compiler_params=pltpu.CompilerParams(
-            collective_id=0, has_side_effects=True, vmem_limit_bytes=60 * 1024 * 1024
+            collective_id=0, has_side_effects=True, vmem_limit_bytes=40 * 1024 * 1024
         ),
     )(owner_map, timestep, latents, stored_sample, table, qkv_weight, out_weight)
 

time: 56.2 us -> 60.2 us (1.071)
  local copies, waits for them, and re-layouts: 1.77 us -> 6.2 us
  Pallas kernels: 51.2 us -> 50.5 us
    unnamed x1 -> x13, local copies, waits for them, and re-layouts: 1.77 us -> 6.2 us
    pallas_call x1, Pallas kernels: 51.2 us -> 50.5 us  [fused(): pl.pallas_call(functools.partial(fused_kernel, groups, cycle, mod_table.s...]
where the time goes in v3:
time: 60.2 us; the launch traced here: 59.9 us
  Pallas kernels  50.5 us (84%)
  local copies, waits for them, and re-layouts  6.2 us (10%)
  between operations  3.12 us (5%)
    pallas_call x1, Pallas kernels, fused(): pl.pallas_call(functools.partial(fused_kernel, groups, cycle, mod_table.s...  50.5 us
    unnamed x13, local copies, waits for them, and re-layouts  6.2 us

profile of v3, /device:TPU:0, one launch (start us, length us, event | category | flops | bytes accessed | tf_op | source)
XLA Modules:
  0.0 59.9 jit_solution(515482456670235736)
XLA Ops:
  1.3 0.0 copy-start.5
  1.3 0.6 %copy-done.5 = s32[8]{0:T(128)S(1)} copy-done((s32[8]{0:T(128)S(1)}, s32[8]{0:T(128)}, u32[]{:S(2)}) %copy-start.5) | copy-done | bytes 56
  1.9 0.0 copy-start
  1.9 1.0 %copy-done = bf16[1,64,3072]{2,1,0:T(8,128)(2,1)S(1)} copy-done((bf16[1,64,3072]{2,1,0:T(8,128)(2,1)S(1)}, bf16[1,64,3072]{2,1,0:T(8,128)(2,1)}, u32[]{:S(2)}) %copy-start) | copy-done | bytes 393240
  2.9 0.0 copy-start.1
  2.9 1.0 %copy-done.1 = bf16[1,64,3072]{2,1,0:T(8,128)(2,1)S(1)} copy-done((bf16[1,64,3072]{2,1,0:T(8,128)(2,1)S(1)}, bf16[1,64,3072]{2,1,0:T(8,128)(2,1)}, u32[]{:S(2)}) %copy-start.1) | copy-done | bytes 393240
  3.9 0.0 copy-start.2
  3.9 1.0 %copy-done.2 = f32[8,3,3072]{2,0,1:T(8,128)S(1)} copy-done((f32[8,3,3072]{2,0,1:T(8,128)S(1)}, f32[8,3,3072]{2,0,1:T(8,128)}, u32[]{:S(2)}) %copy-start.2) | copy-done | bytes 294936
  4.9 0.0 copy-start.3
  4.9 1.0 %copy-done.3 = bf16[384,384]{1,0:T(8,128)(2,1)S(1)} copy-done((bf16[384,384]{1,0:T(8,128)(2,1)S(1)}, bf16[384,384]{1,0:T(8,128)(2,1)}, u32[]{:S(2)}) %copy-start.3) | copy-done | bytes 294936
  5.8 0.0 copy-start.4
  5.9 0.9 %copy-done.4 = bf16[128,384]{1,0:T(8,128)(2,1)S(1)} copy-done((bf16[128,384]{1,0:T(8,128)(2,1)S(1)}, bf16[128,384]{1,0:T(8,128)(2,1)}, u32[]{:S(2)}) %copy-start.4) | copy-done | bytes 98328
  6.7 50.5 %shard_map.86 = (bf16[1,64,3072]{2,1,0:T(8,128)(2,1)S(1)}, f32[1]{0:T(128)}) custom-call(s32[8]{0:T(128)S(1)} %copy-done.5, s32[1]{0:T(128)S(6)} %copy.11.step_ref, bf16[1,64,3072]{2,1,0:T(8,128)(2,1)S(1)} %copy-done, bf16[1,64,3072]{2,1,0:T(8,128)(2,1)S(1)} %copy-done.1, f32[3,8,3072]{2,1,0:T(8,128)S(1)} %bitcast.1, bf16[384,384]{1,0:T(8,128)(2,1)S(1)} %copy-done.3, ...), custom_call_target="tpu_custom_call" | custom-call | tf_op jit(solution)/shard_map/pallas_call | solution.py:350
  57.3 0.7 %copy.12 = bf16[1,64,3072]{2,1,0:T(8,128)(2,1)} copy(bf16[1,64,3072]{2,1,0:T(8,128)(2,1)S(1)} %get-tuple-element.4) | data formatting | bytes 786432
Async XLA Ops:
  1.3 0.7 %copy-start.5 = (s32[8]{0:T(128)S(1)}, s32[8]{0:T(128)}, u32[]{:S(2)}) copy-start(s32[8]{0:T(128)} %owner_ref.1) | copy-start | bytes 100
  1.9 1.0 %copy-start = (bf16[1,64,3072]{2,1,0:T(8,128)(2,1)S(1)}, bf16[1,64,3072]{2,1,0:T(8,128)(2,1)}, u32[]{:S(2)}) copy-start(bf16[1,64,3072]{2,1,0:T(8,128)(2,1)} %lat_hbm.1) | copy-start | bytes 1179652
  2.9 1.0 %copy-start.1 = (bf16[1,64,3072]{2,1,0:T(8,128)(2,1)S(1)}, bf16[1,64,3072]{2,1,0:T(8,128)(2,1)}, u32[]{:S(2)}) copy-start(bf16[1,64,3072]{2,1,0:T(8,128)(2,1)} %sto_hbm.1) | copy-start | bytes 1179652
  3.9 1.0 %copy-start.2 = (f32[8,3,3072]{2,0,1:T(8,128)S(1)}, f32[8,3,3072]{2,0,1:T(8,128)}, u32[]{:S(2)}) copy-start(f32[8,3,3072]{2,0,1:T(8,128)} %param.11) | copy-start | bytes 884740
  4.9 1.0 %copy-start.3 = (bf16[384,384]{1,0:T(8,128)(2,1)S(1)}, bf16[384,384]{1,0:T(8,128)(2,1)}, u32[]{:S(2)}) copy-start(bf16[384,384]{1,0:T(8,128)(2,1)} %wq_hbm.1) | copy-start | bytes 884740
  5.8 0.9 %copy-start.4 = (bf16[128,384]{1,0:T(8,128)(2,1)S(1)}, bf16[128,384]{1,0:T(8,128)(2,1)}, u32[]{:S(2)}) copy-start(bf16[128,384]{1,0:T(8,128)(2,1)} %wo_hbm.1) | copy-start | bytes 294916

commit v4 on v3

--- a/solution.py
+++ b/solution.py
@@ -29,7 +29,8 @@
     lat,
     sto,
     mod,
-    wq,
+    wq_own,
+    wq_edge,
     wo,
     xg,
     qkv,
@@ -41,6 +42,8 @@
     wr,
     zs,
     zr,
+    es,
+    er,
     xs,
     xr,
     as_,
@@ -50,8 +53,13 @@
 ):
     g = lax.axis_index("group")
     t = lax.axis_index("tensor")
-    slices, tok, width = xg.shape[1:]
+    slices, _, width = xg.shape
+    tok = lat.shape[0]
     head_dim = wo.shape[2]
+    top = cycle - 1
+    inner = jnp.logical_and(t > 0, t < top)
+    paired = jnp.logical_or(t == 1, t == top - 1)
+    edge_head = (t - 1) * top // (top - 2)
     chunks = xr.shape[1]
     per_chunk = slices // chunks
     bits = [1 << i for i in range(1, groups.bit_length() - 1)]
@@ -68,7 +76,7 @@
     locals_ = [
         pltpu.make_async_copy(lat_hbm.at[0], lat, local_sem.at[0]),
         pltpu.make_async_copy(mod_hbm, mod, local_sem.at[1]),
-        pltpu.make_async_copy(wq_hbm, wq.at[g], local_sem.at[2]),
+        pltpu.make_async_copy(wq_hbm, wq_own.at[g], local_sem.at[2]),
         pltpu.make_async_copy(wo_hbm, wo.at[g, t], local_sem.at[3]),
         pltpu.make_async_copy(sto_hbm.at[0], sto, local_sem.at[4]),
     ]
@@ -82,17 +90,17 @@
     inv_std = lax.rsqrt(jnp.mean(centred_x * centred_x, axis=-1, keepdims=True) + 1e-06)
     pl.semaphore_wait(barrier, len(partners))
 
-    def piece(payload, head, src_group, half):
-        if payload is None:
-            rows = wq.shape[1] // 2
-            return wq.at[src_group, pl.ds(half * rows, rows)]
-        rows = head_dim // 2
-        return wo.at[src_group, head, pl.ds(half * rows, rows)]
-
-    def plane_copy(head, mask, half, lane, src=None):
-        index = 0 if head is None else 1 + head
+    wq = (wq_own, wq_edge)
+
+    def plane_copy(payload, mask, half, lane, src=None):
+        kind, which = payload
         origin = g ^ mask
-        here = piece(None if head is None else 1, head, origin, half)
+        if kind == "qkv":
+            rows = wq[which].shape[1] // 2
+            index, here = which, wq[which].at[origin, pl.ds(half * rows, rows)]
+        else:
+            rows = head_dim // 2
+            index, here = 2 + which, wo.at[origin, which, pl.ds(half * rows, rows)]
         to = g ^ (1 if lane == 0 else bits[lane - 1])
         return pltpu.make_async_remote_copy(
             src_ref=here if src is None else src,
@@ -108,13 +116,12 @@
         last = max([i for i, b in enumerate(order) if mask & b], default=-1)
         return [bits.index(b) + 1 for b in order[last + 1 :]] + [0]
 
-    def plane_send(head, mask, src_of=None):
-        for half in (0, 1):
-            for lane in lanes_of(mask, half):
-                plane_copy(head, mask, half, lane, src_of and src_of(half)).start()
-
-    def plane_wait(head, mask, half):
-        plane_copy(head, mask, half, 0).wait_recv()
+    def plane_send(payload, mask, half, src=None):
+        for lane in lanes_of(mask, half):
+            plane_copy(payload, mask, half, lane, src).start()
+
+    def plane_wait(payload, mask, half):
+        plane_copy(payload, mask, half, 0).wait_recv()
 
     def plane_partner(head):
         for mask in masks:
@@ -138,9 +145,29 @@
 
     def onward(direction, body):
         if direction == 0:
-            pl.when(t + 1 < cycle)(lambda: body(t + 1))
+            pl.when(t + 1 < top)(lambda: body(t + 1))
         else:
-            pl.when(t - 1 >= 0)(lambda: body(t - 1))
+            pl.when(t - 1 > 0)(lambda: body(t - 1))
+
+    def edge_copy(half, to):
+        rows = wq_edge.shape[1] // 2
+        part_rows = pl.ds(half * rows, rows)
+        return pltpu.make_async_remote_copy(
+            src_ref=wq_hbm.at[part_rows],
+            dst_ref=wq_edge.at[g, part_rows],
+            send_sem=es.at[half],
+            recv_sem=er.at[half],
+            device_id=(g, to),
+            device_id_type=MESH,
+        )
+
+    def from_edge(act):
+        for edge, to in ((0, 1), (top, top - 1)):
+
+            @pl.when(t == edge)
+            def _():
+                for half in (0, 1):
+                    act(edge_copy(half, to))
 
     def head_copy(k):
         here = wo.at[g, t]
@@ -154,7 +181,8 @@
         )
 
     def token_copy(source, direction, k, c, to):
-        here = xg.at[source, pl.ds(c * per_chunk, per_chunk)]
+        rows = pl.ds(pl.multiple_of(source * tok, tok), tok)
+        here = xg.at[pl.ds(c * per_chunk, per_chunk), rows]
         return pltpu.make_async_remote_copy(
             src_ref=here,
             dst_ref=here,
@@ -164,12 +192,19 @@
             device_id_type=MESH,
         )
 
-    half_q = wq.shape[1] // 2
+    half_q = wq_own.shape[1] // 2
     half_o = head_dim // 2
+    from_edge(lambda copy: copy.start())
     for k in range(1, cycle):
         head_copy(k).start()
-    plane_send(None, 0, lambda half: wq_hbm.at[pl.ds(half * half_q, half_q)])
-    plane_send(t, 0, lambda half: wo_hbm.at[pl.ds(half * half_o, half_o)])
+
+    @pl.when(inner)
+    def _():
+        for half in (0, 1):
+            plane_send(("qkv", 0), 0, half, wq_hbm.at[pl.ds(half * half_q, half_q)])
+
+    for half in (0, 1):
+        plane_send(("out", t), 0, half, wo_hbm.at[pl.ds(half * half_o, half_o)])
 
     locals_[1].wait()
     for c in range(chunks):
@@ -179,94 +214,104 @@
             scale = mod[1, pl.ds(time_index, 1), cols]
             shift = mod[0, pl.ds(time_index, 1), cols]
             normed = (piece_x - mean_x) * inv_std
-            xg[t, o] = (normed * (1.0 + scale) + shift).astype(BF16)
+            xg[o, pl.ds(pl.multiple_of(t * tok, tok), tok), :] = (normed * (1.0 + scale) + shift).astype(BF16)
         for direction in (0, 1):
             onward(direction, lambda to, d=direction, c=c: token_copy(t, d, 0, c, to).start())
 
+    def head_of(k):
+        return ("out", lax.rem(t - k + cycle, cycle))
+
     def head_step(k):
         head_copy(k).wait_recv()
-        plane_send(lax.rem(t - k + cycle, cycle), 0)
+        for half in (0, 1):
+            plane_send(head_of(k), 0, half)
+
+    def edge_step(half):
+        @pl.when(paired)
+        def _():
+            edge_copy(half, t).wait_recv()
+            plane_send(("qkv", 1), 0, half)
 
     def token_step(k, c):
         def body(source, direction):
             token_copy(source, direction, k, c, t).wait_recv()
-            if k < cycle - 1:
-                onward(direction, lambda to: token_copy(source, direction, k, c, to).start())
-
-        each_side(k, body)
-
-    def relay(k, mask, half):
-        head = None if k is None else lax.rem(t - k + cycle, cycle)
-        plane_wait(head, mask, half)
-        for lane in lanes_of(mask, half):
-            plane_copy(head, mask, half, lane).start()
-
-    def project(source, wait=None):
-        acc = jnp.zeros((tok, wq.shape[2]), F32)
+            onward(direction, lambda to: token_copy(source, direction, k, c, to).start())
+
+        pl.when(inner)(lambda: each_side(k, body))
+
+    def relay(payload, mask, half, needed=None):
+        def body():
+            plane_wait(payload, mask, half)
+            plane_send(payload, mask, half)
+
+        if needed is None:
+            body()
+        else:
+            pl.when(needed)(body)
+
+    def att_copy(slot, head, k):
+        to = lax.rem(t + k, cycle)
+        return pltpu.make_async_remote_copy(
+            src_ref=att.at[slot, pl.ds(pl.multiple_of(to * tok, tok), tok)],
+            dst_ref=attg.at[head],
+            send_sem=as_.at[slot, k],
+            recv_sem=ar.at[head],
+            device_id=(g, to),
+            device_id_type=MESH,
+        )
+
+    def attend(slot, head):
+        plane_partner(("qkv", slot))
+        acc = jnp.zeros((tok * cycle, wq_own.shape[2]), F32)
         for s in range(slices):
-            if wait is not None and s % per_chunk == 0:
-                wait(s // per_chunk)
-            acc += jnp.dot(xg[source, s], wq[owner_ref[s]], preferred_element_type=F32)
-        qkv[pl.ds(pl.multiple_of(source * tok, tok), tok), :] = acc.astype(BF16)
-
-    events = []
+            acc += jnp.dot(xg[s], wq[slot][owner_ref[s]], preferred_element_type=F32)
+        qkv[...] = acc.astype(BF16)
+        query = qkv[:, :head_dim]
+        key = qkv[:, head_dim : 2 * head_dim]
+        value = qkv[:, 2 * head_dim :]
+        scores = lax.dot_general(
+            query, key, (((1,), (1,)), ((), ())), preferred_element_type=F32
+        ) / math.sqrt(head_dim)
+        expo = jnp.exp(scores - jnp.max(scores, axis=-1, keepdims=True))
+        probs = (expo / jnp.sum(expo, axis=-1, keepdims=True)).astype(BF16)
+        att[slot] = jnp.dot(probs, value, preferred_element_type=F32).astype(BF16)
+        for k in range(1, cycle):
+            att_copy(slot, head, k).start()
+        attg[head] = att[slot, pl.ds(pl.multiple_of(t * tok, tok), tok), :]
+
+    def attend_own():
+        @pl.when(inner)
+        def _():
+            locals_[2].wait()
+            attend(0, t)
+
+    events = [(7.5 + half, functools.partial(edge_step, half)) for half in (0, 1)]
     for k in range(1, cycle):
-        events.append((2 + 2 * k, functools.partial(head_step, k)))
+        events.append((8.7 + 1.1 * k, functools.partial(head_step, k)))
     for k in range(1, cycle - 1):
         for c in range(chunks):
-            events.append((6 + 8 * (k - 1 + c / chunks), functools.partial(token_step, k, c)))
+            events.append((9.5 + 8 * (k - 1 + c / chunks), functools.partial(token_step, k, c)))
     for mask in masks[1:]:
         far = bin(mask).count("1") - 1
         for half in (0, 1):
-            events.append((5 + 2 * half + 6 * far, functools.partial(relay, None, mask, half)))
+            at = 5 + 2 * half + 8 * far
+            events.append((at, functools.partial(relay, ("qkv", 0), mask, half, inner)))
+            at = 12 + 2 * half + 6 * far
+            events.append((at, functools.partial(relay, ("qkv", 1), mask, half, paired)))
             for k in range(cycle):
-                at = 9 + 3 * k + half + 7 * far
-                events.append((at, functools.partial(relay, k, mask, half)))
+                at = 18.1 + 1.5 * k + half / 2 + 7 * far
+                events.append((at, functools.partial(relay, head_of(k), mask, half)))
+    events.append((24.05, attend_own))
+    events.append((26.05, lambda: pl.when(paired)(lambda: attend(1, edge_head))))
     for _, event in sorted(events, key=lambda e: e[0]):
         event()
-    locals_[2].wait()
     locals_[3].wait()
-    plane_partner(None)
-    project(t)
-    for k in range(1, cycle - 1):
-        each_side(k, lambda source, d: project(source))
-    last = cycle - 1
-    each_side(
-        last,
-        lambda source, d: project(
-            source, lambda c: token_copy(source, d, last, c, t).wait_recv()
-        ),
-    )
-
-    query = qkv[:, :head_dim]
-    key = qkv[:, head_dim : 2 * head_dim]
-    value = qkv[:, 2 * head_dim :]
-    scores = lax.dot_general(
-        query, key, (((1,), (1,)), ((), ())), preferred_element_type=F32
-    ) / math.sqrt(head_dim)
-    expo = jnp.exp(scores - jnp.max(scores, axis=-1, keepdims=True))
-    probs = (expo / jnp.sum(expo, axis=-1, keepdims=True)).astype(BF16)
-    att[...] = jnp.dot(probs, value, preferred_element_type=F32).astype(BF16)
-
-    def att_copy(k):
-        to = lax.rem(t + k, cycle)
-        return pltpu.make_async_remote_copy(
-            src_ref=att.at[pl.ds(pl.multiple_of(to * tok, tok), tok)],
-            dst_ref=attg.at[t],
-            send_sem=as_.at[k],
-            recv_sem=ar.at[k],
-            device_id=(g, to),
-            device_id_type=MESH,
-        )
-
-    for k in range(1, cycle):
-        att_copy(k).start()
-    attg[t] = att[pl.ds(pl.multiple_of(t * tok, tok), tok), :]
     for head in range(cycle):
-        plane_partner(head)
+        plane_partner(("out", head))
     locals_[4].wait()
-    for k in range(1, cycle):
-        att_copy(k).wait_recv()
+    for head in range(cycle):
+        home = min(max(head, 1), top - 1)
+        pl.when(t != home)(lambda head=head: att_copy(0, head, 1).wait_recv())
     rows = jnp.concatenate([attg[h] for h in range(cycle)], axis=1)
     time_float = time_index.astype(F32)
     step_size = (time_float + 1.0) / step_count
@@ -298,9 +343,19 @@
 
     for k in range(1, cycle):
         part_copy(k).start()
-    plane_drain(None)
+    def drain_slot(slot, head):
+        plane_drain(("qkv", slot))
+        for k in range(1, cycle):
+            att_copy(slot, head, k).wait_send()
+
+    pl.when(inner)(lambda: drain_slot(0, t))
+    pl.when(paired)(lambda: drain_slot(1, edge_head))
+    pl.when(jnp.logical_not(inner))(locals_[2].wait)
+    from_edge(lambda copy: copy.wait_send())
     for head in range(cycle):
-        plane_drain(head)
+        plane_drain(("out", head))
+    for k in range(1, cycle):
+        head_copy(k).wait_send()
     for direction in (0, 1):
         for c in range(chunks):
             onward(direction, lambda to, d=direction, c=c: token_copy(t, d, 0, c, to).wait_send())
@@ -313,13 +368,10 @@
 
             onward(direction, sent)
 
-        each_side(k, body)
+        pl.when(inner)(lambda: each_side(k, body))
 
     for k in range(1, cycle - 1):
         drain(k)
-    for k in range(1, cycle):
-        head_copy(k).wait_send()
-        att_copy(k).wait_send()
     for k in range(1, cycle):
         part_copy(k).wait_recv()
     total = functools.reduce(lambda a, b: a + b, [part[h] for h in range(cycle)])
@@ -344,7 +396,7 @@
     lanes = groups.bit_length() - 1
     dma = pltpu.SemaphoreType.DMA
     smem = pl.BlockSpec(memory_space=pltpu.SMEM)
-    hbm = pl.BlockSpec(memory_space=pltpu.HBM)
+    anyspace = pl.BlockSpec(memory_space=pl.ANY)
     vmem = pl.BlockSpec(memory_space=pltpu.VMEM)
     table = mod_table.transpose(1, 0, 2)
     return pl.pallas_call(
@@ -353,33 +405,36 @@
             jax.ShapeDtypeStruct((1, tok, model), BF16),
             jax.ShapeDtypeStruct((1,), F32),
         ),
-        in_specs=[smem, smem] + [hbm] * 5,
+        in_specs=[smem, smem] + [anyspace] * 5,
         out_specs=(vmem, smem),
         scratch_shapes=[
             pltpu.VMEM((tok, model), BF16),
             pltpu.VMEM((tok, model), BF16),
             pltpu.VMEM(table.shape, F32),
             pltpu.VMEM((groups, slice_rows, columns), BF16),
+            pltpu.VMEM((groups, slice_rows, columns), BF16),
             pltpu.VMEM((groups, cycle, head_dim, slice_rows), BF16),
-            pltpu.VMEM((cycle, groups, tok, slice_rows), BF16),
+            pltpu.VMEM((groups, cycle * tok, slice_rows), BF16),
             pltpu.VMEM((tok * cycle, columns), BF16),
-            pltpu.VMEM((tok * cycle, head_dim), BF16),
+            pltpu.VMEM((2, tok * cycle, head_dim), BF16),
             pltpu.VMEM((cycle, tok, head_dim), BF16),
             pltpu.VMEM((cycle, 8, 128), F32),
             dma((5,)),
-            dma((1 + cycle, groups // 2, 2, lanes)),
-            dma((1 + cycle, groups, 2)),
+            dma((2 + cycle, groups // 2, 2, lanes)),
+            dma((2 + cycle, groups, 2)),
             dma((cycle,)),
             dma((cycle,)),
+            dma((2,)),
+            dma((2,)),
             dma((2, cycle, chunks)),
             dma((cycle, chunks)),
-            dma((cycle,)),
+            dma((2, cycle)),
             dma((cycle,)),
             dma((cycle,)),
             dma((cycle,)),
         ],
         compiler_params=pltpu.CompilerParams(
-            collective_id=0, has_side_effects=True, vmem_limit_bytes=40 * 1024 * 1024
+            collective_id=0, has_side_effects=True, vmem_limit_bytes=60 * 1024 * 1024
         ),
     )(owner_map, timestep, latents, stored_sample, table, qkv_weight, out_weight)
 
@@ -480,6 +535,7 @@
         head_dim = out_weight.shape[0] // cycle
         fits = (
             samples == groups
+            and cycle >= 4
             and groups & (groups - 1) == 0
             and width % 128 == 0
             and head_dim % 128 == 0

time: 60.2 us -> 56.8 us (0.944)
  local copies, waits for them, and re-layouts: 6.2 us -> 1.77 us
  Pallas kernels: 50.5 us -> 51.8 us
    unnamed x13 -> x1, local copies, waits for them, and re-layouts: 6.2 us -> 1.77 us
    pallas_call x1, Pallas kernels: 50.5 us -> 51.8 us  [fused(): pl.pallas_call(functools.partial(fused_kernel, groups, cycle, mod_table.s...]
where the time goes in v4:
time: 56.8 us; the launch traced here: 56.6 us
  Pallas kernels  51.8 us (91%)
  between operations  3.04 us (5%)
  local copies, waits for them, and re-layouts  1.77 us (3%)
    pallas_call x1, Pallas kernels, fused(): pl.pallas_call(functools.partial(fused_kernel, groups, cycle, mod_table.s...  51.8 us
    unnamed x1, local copies, waits for them, and re-layouts  1.77 us

profile of v4, /device:TPU:0, one launch (start us, length us, event | category | flops | bytes accessed | tf_op | source)
XLA Modules:
  0.0 56.6 jit_solution(14087720799631735260)
XLA Ops:
  1.3 51.8 %shard_map.86 = (bf16[1,64,3072]{2,1,0:T(8,128)(2,1)}, f32[1]{0:T(128)}) custom-call(s32[8]{0:T(128)} %owner_ref.1, s32[1]{0:T(128)S(6)} %copy.11.step_ref, bf16[1,64,3072]{2,1,0:T(8,128)(2,1)} %lat_hbm.1, bf16[1,64,3072]{2,1,0:T(8,128)(2,1)} %sto_hbm.1, f32[3,8,3072]{2,1,0:T(8,128)} %bitcast.1, bf16[384,384]{1,0:T(8,128)(2,1)} %wq_hbm.1, ...), custom_call_target="tpu_custom_call" | custom-call | tf_op jit(solution)/shard_map/pallas_call | solution.py:402
  53.1 1.8 %copy.12 = bf16[1,64,3072]{2,1,0:T(8,128)(2,1)} copy(bf16[1,64,3072]{2,1,0:T(8,128)(2,1)} %get-tuple-element.4) | data formatting | bytes 786432

commit v5 on v3

--- a/solution.py
+++ b/solution.py
@@ -344,7 +344,7 @@
     lanes = groups.bit_length() - 1
     dma = pltpu.SemaphoreType.DMA
     smem = pl.BlockSpec(memory_space=pltpu.SMEM)
-    hbm = pl.BlockSpec(memory_space=pltpu.HBM)
+    anyspace = pl.BlockSpec(memory_space=pl.ANY)
     vmem = pl.BlockSpec(memory_space=pltpu.VMEM)
     table = mod_table.transpose(1, 0, 2)
     return pl.pallas_call(
@@ -353,7 +353,7 @@
             jax.ShapeDtypeStruct((1, tok, model), BF16),
             jax.ShapeDtypeStruct((1,), F32),
         ),
-        in_specs=[smem, smem] + [hbm] * 5,
+        in_specs=[smem, smem] + [anyspace] * 5,
         out_specs=(vmem, smem),
         scratch_shapes=[
             pltpu.VMEM((tok, model), BF16),
@@ -379,7 +379,7 @@
             dma((cycle,)),
         ],
         compiler_params=pltpu.CompilerParams(
-            collective_id=0, has_side_effects=True, vmem_limit_bytes=40 * 1024 * 1024
+            collective_id=0, has_side_effects=True, vmem_limit_bytes=60 * 1024 * 1024
         ),
     )(owner_map, timestep, latents, stored_sample, table, qkv_weight, out_weight)
 
@@ -480,6 +480,7 @@
         head_dim = out_weight.shape[0] // cycle
         fits = (
             samples == groups
+            and cycle >= 4
             and groups & (groups - 1) == 0
             and width % 128 == 0
             and head_dim % 128 == 0

time: 60.2 us -> 56.2 us (0.934)
  local copies, waits for them, and re-layouts: 6.2 us -> 1.77 us
  Pallas kernels: 50.5 us -> 51.2 us
    unnamed x13 -> x1, local copies, waits for them, and re-layouts: 6.2 us -> 1.77 us
    pallas_call x1, Pallas kernels: 50.5 us -> 51.2 us  [fused(): pl.pallas_call(functools.partial(fused_kernel, groups, cycle, mod_table.s...]
where the time goes in v5:
time: 56.2 us; the launch traced here: 56 us
  Pallas kernels  51.2 us (91%)
  between operations  3.04 us (5%)
  local copies, waits for them, and re-layouts  1.77 us (3%)
    pallas_call x1, Pallas kernels, fused(): pl.pallas_call(functools.partial(fused_kernel, groups, cycle, mod_table.s...  51.2 us
    unnamed x1, local copies, waits for them, and re-layouts  1.77 us

profile of v5, /device:TPU:0, one launch (start us, length us, event | category | flops | bytes accessed | tf_op | source)
XLA Modules:
  0.0 56.0 jit_solution(6006047624843941795)
XLA Ops:
  1.3 51.2 %shard_map.86 = (bf16[1,64,3072]{2,1,0:T(8,128)(2,1)}, f32[1]{0:T(128)}) custom-call(s32[8]{0:T(128)} %owner_ref.1, s32[1]{0:T(128)S(6)} %copy.11.step_ref, bf16[1,64,3072]{2,1,0:T(8,128)(2,1)} %lat_hbm.1, bf16[1,64,3072]{2,1,0:T(8,128)(2,1)} %sto_hbm.1, f32[3,8,3072]{2,1,0:T(8,128)} %bitcast.1, bf16[384,384]{1,0:T(8,128)(2,1)} %wq_hbm.1, ...), custom_call_target="tpu_custom_call" | custom-call | tf_op jit(solution)/shard_map/pallas_call | solution.py:350
  52.4 1.8 %copy.12 = bf16[1,64,3072]{2,1,0:T(8,128)(2,1)} copy(bf16[1,64,3072]{2,1,0:T(8,128)(2,1)} %get-tuple-element.4) | data formatting | bytes 786432

commit v6 on v4

--- a/solution.py
+++ b/solution.py
@@ -44,6 +44,7 @@
     zr,
     es,
     er,
+    fs,
     xs,
     xr,
     as_,
@@ -116,9 +117,32 @@
         last = max([i for i, b in enumerate(order) if mask & b], default=-1)
         return [bits.index(b) + 1 for b in order[last + 1 :]] + [0]
 
+    def far_copy(payload, half, to):
+        rows = head_dim // 2
+        here = wo.at[g ^ masks[-1], payload[1], pl.ds(half * rows, rows)]
+        return pltpu.make_async_remote_copy(
+            src_ref=here,
+            dst_ref=here,
+            send_sem=fs.at[payload[1], half],
+            recv_sem=wr.at[2 + payload[1], g ^ masks[-1], half],
+            device_id=(g, to),
+            device_id_type=MESH,
+        )
+
+    def plane_each(payload, mask, half, act, src=None):
+        for lane in lanes_of(mask, half):
+            copy = plane_copy(payload, mask, half, lane, src)
+            far = lane > 0 and (mask | bits[lane - 1]) == masks[-1]
+            if payload[0] == "out" and half == 1 and far:
+                pl.when(jnp.logical_not(paired))(functools.partial(act, copy))
+            else:
+                act(copy)
+        if payload[0] == "out" and half == 1 and mask == masks[-1]:
+            for edge, to in ((0, 1), (top, top - 1)):
+                pl.when(t == edge)(lambda to=to: act(far_copy(payload, half, to)))
+
     def plane_send(payload, mask, half, src=None):
-        for lane in lanes_of(mask, half):
-            plane_copy(payload, mask, half, lane, src).start()
+        plane_each(payload, mask, half, lambda copy: copy.start(), src)
 
     def plane_wait(payload, mask, half):
         plane_copy(payload, mask, half, 0).wait_recv()
@@ -128,11 +152,10 @@
             for half in (0, 1):
                 plane_wait(head, mask | 1, half)
 
-    def plane_drain(head):
+    def plane_drain(payload):
         for mask in masks:
             for half in (0, 1):
-                for lane in lanes_of(mask, half):
-                    plane_copy(head, mask, half, lane).wait_send()
+                plane_each(payload, mask, half, lambda copy: copy.wait_send())
 
     def each_side(k, body):
         @pl.when(t - k >= 0)
@@ -426,6 +449,7 @@
             dma((cycle,)),
             dma((2,)),
             dma((2,)),
+            dma((cycle, 2)),
             dma((2, cycle, chunks)),
             dma((cycle, chunks)),
             dma((2, cycle)),
@@ -535,6 +559,7 @@
         head_dim = out_weight.shape[0] // cycle
         fits = (
             samples == groups
+            and groups >= 4
             and cycle >= 4
             and groups & (groups - 1) == 0
             and width % 128 == 0

time: 56.8 us -> 55.9 us (0.984)
  Pallas kernels: 51.8 us -> 50.9 us
    pallas_call x1, Pallas kernels: 51.8 us -> 50.9 us  [fused(): pl.pallas_call(functools.partial(fused_kernel, groups, cycle, mod_table.s...]
where the time goes in v6:
time: 55.9 us; the launch traced here: 55.7 us
  Pallas kernels  50.9 us (91%)
  between operations  3.04 us (5%)
  local copies, waits for them, and re-layouts  1.77 us (3%)
    pallas_call x1, Pallas kernels, fused(): pl.pallas_call(functools.partial(fused_kernel, groups, cycle, mod_table.s...  50.9 us
    unnamed x1, local copies, waits for them, and re-layouts  1.77 us

profile of v6, /device:TPU:0, one launch (start us, length us, event | category | flops | bytes accessed | tf_op | source)
XLA Modules:
  0.0 55.7 jit_solution(3098144134023441231)
XLA Ops:
  1.3 50.9 %shard_map.86 = (bf16[1,64,3072]{2,1,0:T(8,128)(2,1)}, f32[1]{0:T(128)}) custom-call(s32[8]{0:T(128)} %owner_ref.1, s32[1]{0:T(128)S(6)} %copy.11.step_ref, bf16[1,64,3072]{2,1,0:T(8,128)(2,1)} %lat_hbm.1, bf16[1,64,3072]{2,1,0:T(8,128)(2,1)} %sto_hbm.1, f32[3,8,3072]{2,1,0:T(8,128)} %bitcast.1, bf16[384,384]{1,0:T(8,128)(2,1)} %wq_hbm.1, ...), custom_call_target="tpu_custom_call" | custom-call | tf_op jit(solution)/shard_map/pallas_call | solution.py:425
  52.2 1.8 %copy.12 = bf16[1,64,3072]{2,1,0:T(8,128)(2,1)} copy(bf16[1,64,3072]{2,1,0:T(8,128)(2,1)} %get-tuple-element.4) | data formatting | bytes 786432

commit v7 on v6

--- a/solution.py
+++ b/solution.py
@@ -346,7 +346,7 @@
         latent = lat[:, cols].astype(F32)
         hidden = latent + mod[2, pl.ds(time_index, 1), cols] * proj
         mean = latent - step_size * hidden
-        out_ref[0, :, cols] = mean.astype(BF16)
+        out_ref[0, :, cols] = mean
         residual = sto[:, cols].astype(F32) - mean
         squares += residual * residual
     folded = squares.reshape(tok // 8, 8, width).sum(axis=0)
@@ -422,10 +422,10 @@
     anyspace = pl.BlockSpec(memory_space=pl.ANY)
     vmem = pl.BlockSpec(memory_space=pltpu.VMEM)
     table = mod_table.transpose(1, 0, 2)
-    return pl.pallas_call(
+    mean, log_prob = pl.pallas_call(
         functools.partial(fused_kernel, groups, cycle, mod_table.shape[0]),
         out_shape=(
-            jax.ShapeDtypeStruct((1, tok, model), BF16),
+            jax.ShapeDtypeStruct((1, tok, model), F32),
             jax.ShapeDtypeStruct((1,), F32),
         ),
         in_specs=[smem, smem] + [anyspace] * 5,
@@ -461,6 +461,7 @@
             collective_id=0, has_side_effects=True, vmem_limit_bytes=60 * 1024 * 1024
         ),
     )(owner_map, timestep, latents, stored_sample, table, qkv_weight, out_weight)
+    return mean.astype(BF16), log_prob
 
 
 def shards(latents, stored_sample, timestep, owner_map, mod_table, qkv_weight, out_weight):

time: 55.9 us -> 56.2 us (level)
  other arithmetic: 0 us -> 1.92 us
  local copies, waits for them, and re-layouts: 1.77 us -> 0 us
    convert_element_type x0 -> x1, other arithmetic: none -> 1.92 us  [fused(): return (mean.astype(BF16), log_prob)]
    unnamed x1 -> x0, local copies, waits for them, and re-layouts: 1.77 us -> none
where the time goes in v7:
time: 56.2 us; the launch traced here: 55.9 us
  Pallas kernels  51.1 us (91%)
  between operations  2.96 us (5%)
  other arithmetic  1.92 us (3%)
    pallas_call x1, Pallas kernels, fused(): pl.pallas_call(functools.partial(fused_kernel, groups, cycle, mod_table.s...  51.1 us
    convert_element_type x1, other arithmetic, fused(): return (mean.astype(BF16), log_prob)  1.92 us

profile of v7, /device:TPU:0, one launch (start us, length us, event | category | flops | bytes accessed | tf_op | source)
XLA Modules:
  0.0 55.9 jit_solution(15682069868216052845)
XLA Ops:
  1.3 51.1 %shard_map.86 = (f32[1,64,3072]{2,1,0:T(8,128)}, f32[1]{0:T(128)}) custom-call(s32[8]{0:T(128)} %owner_ref.1, s32[1]{0:T(128)S(6)} %copy.10.step_ref, bf16[1,64,3072]{2,1,0:T(8,128)(2,1)} %lat_hbm.1, bf16[1,64,3072]{2,1,0:T(8,128)(2,1)} %sto_hbm.1, f32[3,8,3072]{2,1,0:T(8,128)} %bitcast.1, bf16[384,384]{1,0:T(8,128)(2,1)} %wq_hbm.1, bf16[128,384]{1,0:T(8,128)(2,1)} %wo_hbm.1), custom_call_target="tpu_custom_call" | custom-call | tf_op jit(solution)/shard_map/pallas_call | solution.py:425
  52.3 1.9 %convert_element_type.3 = bf16[1,64,3072]{2,1,0:T(8,128)(2,1)} convert(f32[1,64,3072]{2,1,0:T(8,128)} %get-tuple-element.4) | non-fusion elementwise | flops 196608 | bytes 1179648 | tf_op jit(solution)/shard_map/convert_element_type | solution.py:464

commit v8 on v6

--- a/solution.py
+++ b/solution.py
@@ -133,11 +133,11 @@
         for lane in lanes_of(mask, half):
             copy = plane_copy(payload, mask, half, lane, src)
             far = lane > 0 and (mask | bits[lane - 1]) == masks[-1]
-            if payload[0] == "out" and half == 1 and far:
+            if payload[0] == "out" and far:
                 pl.when(jnp.logical_not(paired))(functools.partial(act, copy))
             else:
                 act(copy)
-        if payload[0] == "out" and half == 1 and mask == masks[-1]:
+        if payload[0] == "out" and mask == masks[-1]:
             for edge, to in ((0, 1), (top, top - 1)):
                 pl.when(t == edge)(lambda to=to: act(far_copy(payload, half, to)))
 

time: 55.9 us -> 55 us (0.984)
  Pallas kernels: 50.9 us -> 50 us
    pallas_call x1, Pallas kernels: 50.9 us -> 50 us  [fused(): pl.pallas_call(functools.partial(fused_kernel, groups, cycle, mod_table.s...]
where the time goes in v8:
time: 55 us; the launch traced here: 54.8 us
  Pallas kernels  50 us (91%)
  between operations  3.04 us (6%)
  local copies, waits for them, and re-layouts  1.77 us (3%)
    pallas_call x1, Pallas kernels, fused(): pl.pallas_call(functools.partial(fused_kernel, groups, cycle, mod_table.s...  50 us
    unnamed x1, local copies, waits for them, and re-layouts  1.77 us

profile of v8, /device:TPU:0, one launch (start us, length us, event | category | flops | bytes accessed | tf_op | source)
XLA Modules:
  0.0 54.8 jit_solution(1369318963546515208)
XLA Ops:
  1.3 50.0 %shard_map.86 = (bf16[1,64,3072]{2,1,0:T(8,128)(2,1)}, f32[1]{0:T(128)}) custom-call(s32[8]{0:T(128)} %owner_ref.1, s32[1]{0:T(128)S(6)} %copy.11.step_ref, bf16[1,64,3072]{2,1,0:T(8,128)(2,1)} %lat_hbm.1, bf16[1,64,3072]{2,1,0:T(8,128)(2,1)} %sto_hbm.1, f32[3,8,3072]{2,1,0:T(8,128)} %bitcast.1, bf16[384,384]{1,0:T(8,128)(2,1)} %wq_hbm.1, ...), custom_call_target="tpu_custom_call" | custom-call | tf_op jit(solution)/shard_map/pallas_call | solution.py:425
  51.3 1.8 %copy.12 = bf16[1,64,3072]{2,1,0:T(8,128)(2,1)} copy(bf16[1,64,3072]{2,1,0:T(8,128)(2,1)} %get-tuple-element.4) | data formatting | bytes 786432
